TPU v7x, 512 devices: a whole 4x4x16 slice. The times are simulated.
512 devices in a mesh: row: 8 (over y, z_hi), col: 16 (over z_lo, core), rep: 4 (over x).
Axes of the slice: x: 4, y: 4, z: 16 (z_hi: 2, z_lo: 8; z = z_hi * 8 + z_lo), core: 2. Of those that a mesh axis runs over, the one named last changes fastest.
Arguments:
- amplitudes: float32 [18432, 18432], P('row', ('col', 'rep')), may hold values from -0.046875 to 0.046875
- cycle_ints: float32 [18432, 1152], P(('col', 'rep'), 'row'), may hold values from -16 to 16
Outputs:
- cycle_term: float32 [18432, 1152], P(('row', 'rep'), 'col')
All inputs are finite; a program needn't handle non-finite values.
Results may differ from a plain program's by a relative error of at most 0.0002.
Values sent between devices are 32-bit elements; how exact they have to be, the bound alone decides.
A program may use at most 64 MiB of HBM per device.

v0:
```python
import jax
import jax.numpy as jnp
from jax import lax
from jax.sharding import PartitionSpec as P


def passed_along(x, axis, by):
    devices = lax.axis_size(axis)
    return lax.ppermute(x, axis, [(i, (i + by) % devices) for i in range(devices)])


def per_device(amplitudes, cycle_ints):
    n_col = lax.axis_size("col")
    full_ints = lax.all_gather(cycle_ints, "row", axis=1, tiled=True)
    width = full_ints.shape[1] // n_col
    here = lax.axis_index("col")
    n_rows = amplitudes.shape[0]

    def product(block, offset, count):
        columns = lax.dynamic_slice_in_dim(full_ints, block * width + offset, count, 1)
        return jnp.dot(
            amplitudes, columns, precision=lax.Precision.HIGHEST, preferred_element_type=jnp.float32
        )

    def advance(step, partial_sum):
        block = (here - step) % n_col
        partial_sum = partial_sum + product(block, 0, width)
        return passed_along(partial_sum, "col", 1)

    totals = lax.fori_loop(0, n_col, advance, jnp.zeros((n_rows, width), jnp.float32))
    return lax.psum_scatter(totals, "rep", scatter_dimension=0, tiled=True)


def solution(mesh):
    return jax.shard_map(
        per_device,
        mesh=mesh,
        in_specs=(P("row", ("col", "rep")), P(("col", "rep"), "row")),
        out_specs=P(("row", "rep"), "col"),
        check_vma=False,
    )
```

profile of v0, /device:TPU:8, one launch (start us, length us, event | category | flops | bytes accessed | tf_op | source)
XLA Modules:
  0.0 518.8 jit_solution(9716333784777481202)
XLA Ops:
  7.3 116.8 %all-gather.2.cloned.1.call-done = f32[288,1152]{0,1:T(8,128)} async-done(((f32[288,144]{0,1:T(8,128)}), f32[288,1152]{0,1:T(8,128)}) %all-gather.2.cloned.1.call-update) | async-done | bytes 1327120 | tf_op jit(solution)/shard_map/all_gather | solution.py:14
  124.1 360.7 %while.15 = (s32[]{:T(128)}, f32[2304,72]{0,1:T(8,128)S(1)}, s32[]{:T(128)}, f32[288,1152]{0,1:T(8,128)}, f32[2304,288]{0,1:T(8,128)}, /*index=5*/s32[]{:T(128)}...) while((s32[]{:T(128)}, f32[2304,72]{0,1:T(8,128)S(1)}, s32[]{:T(128)}, ...), condition=%wide.region_1.2_spmd, body=%wide.region_0.1_spmd.sunk | while | flops 573474816 | bytes 6746432 | solution.py:30
  124.2 3.9 fusion.9
  130.0 16.7 %collective-permute-done = f32[2304,72]{0,1:T(8,128)S(1)} collective-permute-done((f32[2304,72]{0,1:T(8,128)S(1)}, f32[2304,72]{0,1:T(8,128)S(1)}, u32[]{:S(2)}, u32[]{:S(2)}) %collective-permute-start) | collective-permute-done | bytes 663584 | tf_op jit(solution)/shard_map/while/body/eval_jaxpr/ppermute | solution.py:9
  146.7 3.9 fusion.9
  152.6 16.7 %collective-permute-done = f32[2304,72]{0,1:T(8,128)S(1)} collective-permute-done((f32[2304,72]{0,1:T(8,128)S(1)}, f32[2304,72]{0,1:T(8,128)S(1)}, u32[]{:S(2)}, u32[]{:S(2)}) %collective-permute-start) | collective-permute-done | bytes 663584 | tf_op jit(solution)/shard_map/while/body/eval_jaxpr/ppermute | solution.py:9
  169.3 3.9 fusion.9
  175.1 16.7 %collective-permute-done = f32[2304,72]{0,1:T(8,128)S(1)} collective-permute-done((f32[2304,72]{0,1:T(8,128)S(1)}, f32[2304,72]{0,1:T(8,128)S(1)}, u32[]{:S(2)}, u32[]{:S(2)}) %collective-permute-start) | collective-permute-done | bytes 663584 | tf_op jit(solution)/shard_map/while/body/eval_jaxpr/ppermute | solution.py:9
  191.8 3.9 fusion.9
  197.7 16.7 %collective-permute-done = f32[2304,72]{0,1:T(8,128)S(1)} collective-permute-done((f32[2304,72]{0,1:T(8,128)S(1)}, f32[2304,72]{0,1:T(8,128)S(1)}, u32[]{:S(2)}, u32[]{:S(2)}) %collective-permute-start) | collective-permute-done | bytes 663584 | tf_op jit(solution)/shard_map/while/body/eval_jaxpr/ppermute | solution.py:9
  214.3 3.9 fusion.9
  220.2 16.7 %collective-permute-done = f32[2304,72]{0,1:T(8,128)S(1)} collective-permute-done((f32[2304,72]{0,1:T(8,128)S(1)}, f32[2304,72]{0,1:T(8,128)S(1)}, u32[]{:S(2)}, u32[]{:S(2)}) %collective-permute-start) | collective-permute-done | bytes 663584 | tf_op jit(solution)/shard_map/while/body/eval_jaxpr/ppermute | solution.py:9
  242.8 16.7 %collective-permute-done = f32[2304,72]{0,1:T(8,128)S(1)} collective-permute-done((f32[2304,72]{0,1:T(8,128)S(1)}, f32[2304,72]{0,1:T(8,128)S(1)}, u32[]{:S(2)}, u32[]{:S(2)}) %collective-permute-start) | collective-permute-done | bytes 663584 | tf_op jit(solution)/shard_map/while/body/eval_jaxpr/ppermute | solution.py:9
  265.3 16.7 %collective-permute-done = f32[2304,72]{0,1:T(8,128)S(1)} collective-permute-done((f32[2304,72]{0,1:T(8,128)S(1)}, f32[2304,72]{0,1:T(8,128)S(1)}, u32[]{:S(2)}, u32[]{:S(2)}) %collective-permute-start) | collective-permute-done | bytes 663584 | tf_op jit(solution)/shard_map/while/body/eval_jaxpr/ppermute | solution.py:9
  287.8 16.7 %collective-permute-done = f32[2304,72]{0,1:T(8,128)S(1)} collective-permute-done((f32[2304,72]{0,1:T(8,128)S(1)}, f32[2304,72]{0,1:T(8,128)S(1)}, u32[]{:S(2)}, u32[]{:S(2)}) %collective-permute-start) | collective-permute-done | bytes 663584 | tf_op jit(solution)/shard_map/while/body/eval_jaxpr/ppermute | solution.py:9
  310.4 16.7 %collective-permute-done = f32[2304,72]{0,1:T(8,128)S(1)} collective-permute-done((f32[2304,72]{0,1:T(8,128)S(1)}, f32[2304,72]{0,1:T(8,128)S(1)}, u32[]{:S(2)}, u32[]{:S(2)}) %collective-permute-start) | collective-permute-done | bytes 663584 | tf_op jit(solution)/shard_map/while/body/eval_jaxpr/ppermute | solution.py:9
  332.9 16.7 %collective-permute-done = f32[2304,72]{0,1:T(8,128)S(1)} collective-permute-done((f32[2304,72]{0,1:T(8,128)S(1)}, f32[2304,72]{0,1:T(8,128)S(1)}, u32[]{:S(2)}, u32[]{:S(2)}) %collective-permute-start) | collective-permute-done | bytes 663584 | tf_op jit(solution)/shard_map/while/body/eval_jaxpr/ppermute | solution.py:9
  355.5 16.7 %collective-permute-done = f32[2304,72]{0,1:T(8,128)S(1)} collective-permute-done((f32[2304,72]{0,1:T(8,128)S(1)}, f32[2304,72]{0,1:T(8,128)S(1)}, u32[]{:S(2)}, u32[]{:S(2)}) %collective-permute-start) | collective-permute-done | bytes 663584 | tf_op jit(solution)/shard_map/while/body/eval_jaxpr/ppermute | solution.py:9
  378.0 16.7 %collective-permute-done = f32[2304,72]{0,1:T(8,128)S(1)} collective-permute-done((f32[2304,72]{0,1:T(8,128)S(1)}, f32[2304,72]{0,1:T(8,128)S(1)}, u32[]{:S(2)}, u32[]{:S(2)}) %collective-permute-start) | collective-permute-done | bytes 663584 | tf_op jit(solution)/shard_map/while/body/eval_jaxpr/ppermute | solution.py:9
  400.6 16.7 %collective-permute-done = f32[2304,72]{0,1:T(8,128)S(1)} collective-permute-done((f32[2304,72]{0,1:T(8,128)S(1)}, f32[2304,72]{0,1:T(8,128)S(1)}, u32[]{:S(2)}, u32[]{:S(2)}) %collective-permute-start) | collective-permute-done | bytes 663584 | tf_op jit(solution)/shard_map/while/body/eval_jaxpr/ppermute | solution.py:9
  423.1 16.7 %collective-permute-done = f32[2304,72]{0,1:T(8,128)S(1)} collective-permute-done((f32[2304,72]{0,1:T(8,128)S(1)}, f32[2304,72]{0,1:T(8,128)S(1)}, u32[]{:S(2)}, u32[]{:S(2)}) %collective-permute-start) | collective-permute-done | bytes 663584 | tf_op jit(solution)/shard_map/while/body/eval_jaxpr/ppermute | solution.py:9
  445.6 16.7 %collective-permute-done = f32[2304,72]{0,1:T(8,128)S(1)} collective-permute-done((f32[2304,72]{0,1:T(8,128)S(1)}, f32[2304,72]{0,1:T(8,128)S(1)}, u32[]{:S(2)}, u32[]{:S(2)}) %collective-permute-start) | collective-permute-done | bytes 663584 | tf_op jit(solution)/shard_map/while/body/eval_jaxpr/ppermute | solution.py:9
  468.2 16.7 %collective-permute-done = f32[2304,72]{0,1:T(8,128)S(1)} collective-permute-done((f32[2304,72]{0,1:T(8,128)S(1)}, f32[2304,72]{0,1:T(8,128)S(1)}, u32[]{:S(2)}, u32[]{:S(2)}) %collective-permute-start) | collective-permute-done | bytes 663584 | tf_op jit(solution)/shard_map/while/body/eval_jaxpr/ppermute | solution.py:9
  486.3 23.9 %reduce-scatter.4.cloned.1.call-done = f32[576,72]{1,0:T(8,128)} async-done(((f32[2304,72]{1,0:T(8,128)}), f32[576,72]{1,0:T(8,128)}) %reduce-scatter.4.cloned.1.call-update) | async-done | bytes 165904
  (34 shorter events, 78.0 us)
Async XLA Ops:
  6.5 117.5 %all-gather.2.cloned.1.call-start = ((), (), s32[]{:S(2)}) async-start(), calls=%async_computation.1 | async-start | bytes 1990656 | tf_op jit(solution)/shard_map/all_gather | solution.py:14
  7.3 502.9 %reduce-scatter.4.cloned.1.call-start = ((), (), s32[]{:S(2)}) async-start(), calls=%async_computation.2 | async-start | bytes 1474560
  128.1 18.6 %collective-permute-start = (f32[2304,72]{0,1:T(8,128)S(1)}, f32[2304,72]{0,1:T(8,128)S(1)}, u32[]{:S(2)}, u32[]{:S(2)}) collective-permute-start(f32[2304,72]{0,1:T(8,128)S(1)} %fusion.9), channel_id=1, source_target_pairs={{0,4},{4,8},{8,12},{12,16},{16,20},{20,24},{24,28},{28,32},{32,36}... | collective-permute-start | bytes 1990664 | tf_op jit(solution)/shard_map/while/body/eval_jaxpr/ppermute | solution.py:9
  150.7 18.6 %collective-permute-start = (f32[2304,72]{0,1:T(8,128)S(1)}, f32[2304,72]{0,1:T(8,128)S(1)}, u32[]{:S(2)}, u32[]{:S(2)}) collective-permute-start(f32[2304,72]{0,1:T(8,128)S(1)} %fusion.9), channel_id=1, source_target_pairs={{0,4},{4,8},{8,12},{12,16},{16,20},{20,24},{24,28},{28,32},{32,36}... | collective-permute-start | bytes 1990664 | tf_op jit(solution)/shard_map/while/body/eval_jaxpr/ppermute | solution.py:9
  173.2 18.6 %collective-permute-start = (f32[2304,72]{0,1:T(8,128)S(1)}, f32[2304,72]{0,1:T(8,128)S(1)}, u32[]{:S(2)}, u32[]{:S(2)}) collective-permute-start(f32[2304,72]{0,1:T(8,128)S(1)} %fusion.9), channel_id=1, source_target_pairs={{0,4},{4,8},{8,12},{12,16},{16,20},{20,24},{24,28},{28,32},{32,36}... | collective-permute-start | bytes 1990664 | tf_op jit(solution)/shard_map/while/body/eval_jaxpr/ppermute | solution.py:9
  195.7 18.6 %collective-permute-start = (f32[2304,72]{0,1:T(8,128)S(1)}, f32[2304,72]{0,1:T(8,128)S(1)}, u32[]{:S(2)}, u32[]{:S(2)}) collective-permute-start(f32[2304,72]{0,1:T(8,128)S(1)} %fusion.9), channel_id=1, source_target_pairs={{0,4},{4,8},{8,12},{12,16},{16,20},{20,24},{24,28},{28,32},{32,36}... | collective-permute-start | bytes 1990664 | tf_op jit(solution)/shard_map/while/body/eval_jaxpr/ppermute | solution.py:9
  218.3 18.6 %collective-permute-start = (f32[2304,72]{0,1:T(8,128)S(1)}, f32[2304,72]{0,1:T(8,128)S(1)}, u32[]{:S(2)}, u32[]{:S(2)}) collective-permute-start(f32[2304,72]{0,1:T(8,128)S(1)} %fusion.9), channel_id=1, source_target_pairs={{0,4},{4,8},{8,12},{12,16},{16,20},{20,24},{24,28},{28,32},{32,36}... | collective-permute-start | bytes 1990664 | tf_op jit(solution)/shard_map/while/body/eval_jaxpr/ppermute | solution.py:9
  240.8 18.6 %collective-permute-start = (f32[2304,72]{0,1:T(8,128)S(1)}, f32[2304,72]{0,1:T(8,128)S(1)}, u32[]{:S(2)}, u32[]{:S(2)}) collective-permute-start(f32[2304,72]{0,1:T(8,128)S(1)} %fusion.9), channel_id=1, source_target_pairs={{0,4},{4,8},{8,12},{12,16},{16,20},{20,24},{24,28},{28,32},{32,36}... | collective-permute-start | bytes 1990664 | tf_op jit(solution)/shard_map/while/body/eval_jaxpr/ppermute | solution.py:9
  263.4 18.6 %collective-permute-start = (f32[2304,72]{0,1:T(8,128)S(1)}, f32[2304,72]{0,1:T(8,128)S(1)}, u32[]{:S(2)}, u32[]{:S(2)}) collective-permute-start(f32[2304,72]{0,1:T(8,128)S(1)} %fusion.9), channel_id=1, source_target_pairs={{0,4},{4,8},{8,12},{12,16},{16,20},{20,24},{24,28},{28,32},{32,36}... | collective-permute-start | bytes 1990664 | tf_op jit(solution)/shard_map/while/body/eval_jaxpr/ppermute | solution.py:9
  285.9 18.6 %collective-permute-start = (f32[2304,72]{0,1:T(8,128)S(1)}, f32[2304,72]{0,1:T(8,128)S(1)}, u32[]{:S(2)}, u32[]{:S(2)}) collective-permute-start(f32[2304,72]{0,1:T(8,128)S(1)} %fusion.9), channel_id=1, source_target_pairs={{0,4},{4,8},{8,12},{12,16},{16,20},{20,24},{24,28},{28,32},{32,36}... | collective-permute-start | bytes 1990664 | tf_op jit(solution)/shard_map/while/body/eval_jaxpr/ppermute | solution.py:9
  308.5 18.6 %collective-permute-start = (f32[2304,72]{0,1:T(8,128)S(1)}, f32[2304,72]{0,1:T(8,128)S(1)}, u32[]{:S(2)}, u32[]{:S(2)}) collective-permute-start(f32[2304,72]{0,1:T(8,128)S(1)} %fusion.9), channel_id=1, source_target_pairs={{0,4},{4,8},{8,12},{12,16},{16,20},{20,24},{24,28},{28,32},{32,36}... | collective-permute-start | bytes 1990664 | tf_op jit(solution)/shard_map/while/body/eval_jaxpr/ppermute | solution.py:9
  331.0 18.6 %collective-permute-start = (f32[2304,72]{0,1:T(8,128)S(1)}, f32[2304,72]{0,1:T(8,128)S(1)}, u32[]{:S(2)}, u32[]{:S(2)}) collective-permute-start(f32[2304,72]{0,1:T(8,128)S(1)} %fusion.9), channel_id=1, source_target_pairs={{0,4},{4,8},{8,12},{12,16},{16,20},{20,24},{24,28},{28,32},{32,36}... | collective-permute-start | bytes 1990664 | tf_op jit(solution)/shard_map/while/body/eval_jaxpr/ppermute | solution.py:9
  353.5 18.6 %collective-permute-start = (f32[2304,72]{0,1:T(8,128)S(1)}, f32[2304,72]{0,1:T(8,128)S(1)}, u32[]{:S(2)}, u32[]{:S(2)}) collective-permute-start(f32[2304,72]{0,1:T(8,128)S(1)} %fusion.9), channel_id=1, source_target_pairs={{0,4},{4,8},{8,12},{12,16},{16,20},{20,24},{24,28},{28,32},{32,36}... | collective-permute-start | bytes 1990664 | tf_op jit(solution)/shard_map/while/body/eval_jaxpr/ppermute | solution.py:9
  376.1 18.6 %collective-permute-start = (f32[2304,72]{0,1:T(8,128)S(1)}, f32[2304,72]{0,1:T(8,128)S(1)}, u32[]{:S(2)}, u32[]{:S(2)}) collective-permute-start(f32[2304,72]{0,1:T(8,128)S(1)} %fusion.9), channel_id=1, source_target_pairs={{0,4},{4,8},{8,12},{12,16},{16,20},{20,24},{24,28},{28,32},{32,36}... | collective-permute-start | bytes 1990664 | tf_op jit(solution)/shard_map/while/body/eval_jaxpr/ppermute | solution.py:9
  398.6 18.6 %collective-permute-start = (f32[2304,72]{0,1:T(8,128)S(1)}, f32[2304,72]{0,1:T(8,128)S(1)}, u32[]{:S(2)}, u32[]{:S(2)}) collective-permute-start(f32[2304,72]{0,1:T(8,128)S(1)} %fusion.9), channel_id=1, source_target_pairs={{0,4},{4,8},{8,12},{12,16},{16,20},{20,24},{24,28},{28,32},{32,36}... | collective-permute-start | bytes 1990664 | tf_op jit(solution)/shard_map/while/body/eval_jaxpr/ppermute | solution.py:9
  421.2 18.6 %collective-permute-start = (f32[2304,72]{0,1:T(8,128)S(1)}, f32[2304,72]{0,1:T(8,128)S(1)}, u32[]{:S(2)}, u32[]{:S(2)}) collective-permute-start(f32[2304,72]{0,1:T(8,128)S(1)} %fusion.9), channel_id=1, source_target_pairs={{0,4},{4,8},{8,12},{12,16},{16,20},{20,24},{24,28},{28,32},{32,36}... | collective-permute-start | bytes 1990664 | tf_op jit(solution)/shard_map/while/body/eval_jaxpr/ppermute | solution.py:9
  443.7 18.6 %collective-permute-start = (f32[2304,72]{0,1:T(8,128)S(1)}, f32[2304,72]{0,1:T(8,128)S(1)}, u32[]{:S(2)}, u32[]{:S(2)}) collective-permute-start(f32[2304,72]{0,1:T(8,128)S(1)} %fusion.9), channel_id=1, source_target_pairs={{0,4},{4,8},{8,12},{12,16},{16,20},{20,24},{24,28},{28,32},{32,36}... | collective-permute-start | bytes 1990664 | tf_op jit(solution)/shard_map/while/body/eval_jaxpr/ppermute | solution.py:9
  466.3 18.6 %collective-permute-start = (f32[2304,72]{0,1:T(8,128)S(1)}, f32[2304,72]{0,1:T(8,128)S(1)}, u32[]{:S(2)}, u32[]{:S(2)}) collective-permute-start(f32[2304,72]{0,1:T(8,128)S(1)} %fusion.9), channel_id=1, source_target_pairs={{0,4},{4,8},{8,12},{12,16},{16,20},{20,24},{24,28},{28,32},{32,36}... | collective-permute-start | bytes 1990664 | tf_op jit(solution)/shard_map/while/body/eval_jaxpr/ppermute | solution.py:9
Sparse Core Ops, SparseCore 0:
  10.5 113.4 all-gather.1
  486.4 23.7 reduce-scatter.3
where the time goes:
time: 520 us; the launch traced here: 519 us
  waiting for transfers between devices  408 us (78%)
  matrix products  63 us (12%)
  starting transfers between devices  30.8 us (6%)
  between operations  13.4 us (3%)
    ppermute x16, waiting for transfers between devices, passed_along(): lax.ppermute(x, axis, [(i, (i + by) % devices) for i in range(devices)])  267 us
    all_gather x1, waiting for transfers between devices, per_device(): full_ints = lax.all_gather(cycle_ints, 'row', axis=1, tiled=True)  117 us
    dot_general x16, matrix products, product(): jnp.dot(amplitudes, columns, precision=lax.Precision.HIGHEST, preferred_e...  63 us
    ppermute x16, starting transfers between devices, passed_along(): lax.ppermute(x, axis, [(i, (i + by) % devices) for i in range(devices)])  30.7 us
    unnamed x3, waiting for transfers between devices  24.6 us
  transfers between devices with their start and end apart: 18, of which 18 were waited for; matrix products, arithmetic and copies ran while one was open for 0% of the time, Pallas kernels for 0%

commit v1 on v0

v1 whole, which is shorter than its diff:
```python
import functools

import jax
import jax.numpy as jnp
from jax import lax
from jax.experimental import pallas as pl
from jax.experimental.pallas import tpu as pltpu
from jax.sharding import PartitionSpec as P

MESH = pl.DeviceIdType.MESH
STEPS = 8
NX = 4
TOP = 160
UNIT = 328
BOT = UNIT - TOP
LAG = 2


def split(value):
    high = value.astype(jnp.bfloat16)
    return high, (value - high.astype(jnp.float32)).astype(jnp.bfloat16)


def kernel(
    at_ref, bt_ref, out_ref,
    a_own, a_oth, ah, al, b_own, b_oth, bq, pu, opp_l, opp_r, in_l, in_r, z_l, z_r,
    loc_sem, core_s, core_r, b_s, b_r, x_s, x_r, z_s, z_rs,
):
    row, col, x = lax.axis_index("row"), lax.axis_index("col"), lax.axis_index("rep")
    y, h = row // 2, row % 2
    z, c = col // 2, col % 2
    other = {"col": col + 1 - 2 * c}
    right, left, opp = (x + 1) % NX, (x + 3) % NX, (x + 2) % NX
    to_right, to_left = {"rep": right}, {"rep": left}
    twin_row = row + 1 - 2 * h
    y_rows = [(row + 2) % 8, (row + 6) % 8, (row + 4) % 8]

    load_a = [
        pltpu.make_async_copy(
            at_ref.at[:, pl.ds(1152 * p, 1152)], a_own.at[:, pl.ds(1152 * p, 1152)], loc_sem.at[p]
        )
        for p in range(2)
    ]
    load_b = pltpu.make_async_copy(bt_ref, b_own, loc_sem.at[2])
    load_b.start()
    for cp in load_a:
        cp.start()

    barrier = pltpu.get_barrier_semaphore()

    def greet(device):
        pl.semaphore_signal(barrier, inc=1, device_id=device, device_id_type=MESH)

    greet(other)
    greet(to_right)
    greet(to_left)
    for r in y_rows:
        greet({"row": r})
    greet({"row": twin_row})

    @pl.when(z > 0)
    def _():
        greet({"col": col - 2})

    @pl.when(z < 7)
    def _():
        greet({"col": col + 2})

    pl.semaphore_wait(barrier, 7 + jnp.minimum(z, 1) + jnp.minimum(7 - z, 1))

    load_b.wait()
    swap_b = pltpu.make_async_remote_copy(
        b_own.at[pl.ds((1 - c) * 72, 72)], b_oth, core_s.at[0], core_r.at[0],
        device_id=other, device_id_type=MESH,
    )
    swap_b.start()
    swap_a = []
    for p in range(2):
        load_a[p].wait()
        cp = pltpu.make_async_remote_copy(
            a_own.at[:, pl.ds(1152 * p, 1152)], a_oth.at[:, pl.ds(1152 * p, 1152)],
            core_s.at[1 + p], core_r.at[1 + p], device_id=other, device_id_type=MESH,
        )
        cp.start()
        swap_a.append(cp)
    swap_b.wait_recv()
    bq[row, :, 0:576] = jnp.concatenate([b_own[pl.ds(c * 72, 72), :], b_oth[...]], axis=1)

    def send_b(slot, target, sem):
        return pltpu.make_async_remote_copy(
            bq.at[slot], bq.at[slot], b_s.at[sem], b_r.at[slot],
            device_id={"row": target}, device_id_type=MESH,
        )

    sends_b = [send_b(row, twin_row, 0)]
    sends_b += [send_b(row, r, 1 + n) for n, r in enumerate(y_rows)]
    for cp in sends_b:
        cp.start()
    relays_b = [send_b(twin_row, r, 4 + n) for n, r in enumerate(y_rows)]

    def convert(source, base):
        def some(i, _):
            rows = pl.ds(pl.multiple_of(i * 16, 16), 16)
            into = pl.ds(pl.multiple_of(base + i * 16, 16), 16)
            high, low = split(source[rows, :])
            ah[into, :] = high
            al[into, :] = low
            return 0

        lax.fori_loop(0, 18, some, 0, unroll=3)

    convert(a_own, 0)
    for cp in swap_a:
        cp.wait_recv()
    convert(a_oth, 288)

    def order(i):
        near = i + (i // 2) * (1 - 2 * (i % 2))
        first = 2 * ((y + near) % 4) + h
        j = i - 4
        base = (j % 2) * (7 - j) + (1 - j % 2) * j
        last = (1 - h) * 7 + (1 - 2 * (1 - h)) * base
        return jnp.where(i < 4, first, last)

    lanes = lax.broadcasted_iota(jnp.int32, (40, 128), 1)

    def x_copy(kind, i):
        top, bot = pl.ds(0, TOP), pl.ds(TOP, BOT)
        src, dst, device = (
            (pu.at[i, opp, top], opp_l.at[i], to_right),
            (pu.at[i, opp, bot], opp_r.at[i], to_left),
            (pu.at[i, right, bot], in_l.at[i, bot], to_right),
            (pu.at[i, left, top], in_r.at[i, top], to_left),
            (pu.at[i, right, top], in_l.at[i, top], to_right),
            (pu.at[i, left, bot], in_r.at[i, bot], to_left),
        )[kind]
        return pltpu.make_async_remote_copy(
            src, dst, x_s.at[kind, i], x_r.at[kind, i], device_id=device, device_id_type=MESH
        )

    def z_copy(up, i):
        return pltpu.make_async_remote_copy(
            pu.at[i, x], (z_l if up else z_r).at[i],
            z_s.at[0, i], z_rs.at[0 if up else 1, i],
            device_id={"col": col + 2 if up else col - 2}, device_id_type=MESH,
        )

    def product(i):
        d = order(i)

        @pl.when((d != row) & (d != twin_row))
        def _():
            send_b(d, twin_row, 0).wait_recv()

        bh, bl = split(bq[d, :, 0:576])
        for n in range(2):
            p = x // 2 if n else 1 - x // 2
            span = pl.ds(pl.multiple_of(1152 * p, 128), 1152)
            high = ah[:, span]
            v = jnp.dot(bh, high, preferred_element_type=jnp.float32)
            v += jnp.dot(bl, high, preferred_element_type=jnp.float32)
            v += jnp.dot(bh, al[:, span], preferred_element_type=jnp.float32)
            for j in range(4):
                pu[i, 2 * p, 72 * j:72 * j + 72, :] = v[:, 128 * j:128 * j + 128]
                pu[i, 2 * p + 1, 72 * j:72 * j + 72, :] = v[:, 640 + 128 * j:768 + 128 * j]
            up, down = v[0:40, 512:640], v[32:72, 512:640]
            pu[i, 2 * p, 288:328, :] = jnp.where(lanes < 64, up, pltpu.roll(down, 64, 1))
            pu[i, 2 * p + 1, 288:328, :] = jnp.where(lanes < 64, pltpu.roll(up, 64, 1), down)
            if n == 0:
                x_copy(0, i).start()
                x_copy(1, i).start()
        x_copy(2, i).start()
        x_copy(3, i).start()

    def relay(i):
        x_copy(0, i).wait_recv()
        pu[i, right, 0:TOP, :] += opp_l[i]
        x_copy(4, i).start()
        x_copy(1, i).wait_recv()
        pu[i, left, TOP:UNIT, :] += opp_r[i]
        x_copy(5, i).start()

    def gather(i):
        for kind in (2, 4, 3, 5):
            x_copy(kind, i).wait_recv()
        pu[i, x] += in_l[i] + in_r[i]

    def write_out(i):
        v = [pu[i, x, 72 * j:72 * j + 72, :] for j in range(4)]
        tail = pu[i, x, 288:328, :]
        turned = pltpu.roll(tail, 64, 1)
        tail = jnp.concatenate([tail, turned[8:40]], axis=0)

        @pl.when(x % 2 == 0)
        def _():
            for j in range(4):
                out_ref[:, 128 * j:128 * j + 128] = v[j]
            out_ref[:, 512:576] = tail[:, 0:64]

        @pl.when(x % 2 == 1)
        def _():
            r = [pltpu.roll(w, 64, 1) for w in v]
            low = lax.broadcasted_iota(jnp.int32, (72, 128), 1) < 64
            out_ref[:, 0:128] = jnp.where(low, tail, r[0])
            for j in range(1, 4):
                out_ref[:, 128 * j:128 * j + 128] = jnp.where(low, r[j - 1], r[j])
            out_ref[:, 512:576] = r[3][:, 0:64]

    def valid(i):
        return (i >= 0) & (i < STEPS)

    def step(s, _):
        @pl.when(valid(s))
        def _():
            product(s)

        @pl.when(valid(s - 1))
        def _():
            relay(s - 1)

        @pl.when(s == 2)
        def _():
            send_b(twin_row, y_rows[0], 0).wait_recv()
            for cp in relays_b:
                cp.start()

        @pl.when(valid(s - 2))
        def _():
            gather(s - 2)

        i = s - LAG - z
        d = order(i)

        @pl.when(valid(i) & (d >= z))
        def _():
            @pl.when(z > 0)
            def _():
                z_copy(True, i).wait_recv()
                pu[i, x] += z_l[i]

            @pl.when(d > z)
            def _():
                z_copy(True, i).start()

        k = s - LAG - (7 - z)
        e = order(k)

        @pl.when(valid(k) & (e <= z))
        def _():
            @pl.when(z < 7)
            def _():
                z_copy(False, k).wait_recv()
                pu[k, x] += z_r[k]

            @pl.when(e < z)
            def _():
                z_copy(False, k).start()

        return 0

    lax.fori_loop(0, STEPS + LAG + 4, step, 0)

    def find(i, _):
        @pl.when(order(i) == z)
        def _():
            write_out(i)

        return 0

    lax.fori_loop(0, STEPS, find, 0)

    def drain(i, _):
        for kind in range(6):
            x_copy(kind, i).wait_send()

        @pl.when(order(i) != z)
        def _():
            z_copy(True, i).wait_send()

        return 0

    lax.fori_loop(0, STEPS, drain, 0)
    swap_b.wait_send()
    for cp in swap_a:
        cp.wait_send()
    for cp in sends_b + relays_b:
        cp.wait_send()


def per_device(amplitudes, cycle_ints):
    f32 = jnp.float32
    out = pl.pallas_call(
        kernel,
        out_shape=jax.ShapeDtypeStruct((72, 576), f32),
        in_specs=[pl.BlockSpec(memory_space=pl.ANY)] * 2,
        out_specs=pl.BlockSpec(memory_space=pltpu.VMEM),
        scratch_shapes=[
            pltpu.VMEM((288, 2304), f32),
            pltpu.VMEM((288, 2304), f32),
            pltpu.VMEM((576, 2304), jnp.bfloat16),
            pltpu.VMEM((576, 2304), jnp.bfloat16),
            pltpu.VMEM((144, 288), f32),
            pltpu.VMEM((72, 288), f32),
            pltpu.VMEM((8, 72, 640), f32),
            pltpu.VMEM((STEPS, NX, UNIT, 128), f32),
            pltpu.VMEM((STEPS, TOP, 128), f32),
            pltpu.VMEM((STEPS, BOT, 128), f32),
            pltpu.VMEM((STEPS, UNIT, 128), f32),
            pltpu.VMEM((STEPS, UNIT, 128), f32),
            pltpu.VMEM((STEPS, UNIT, 128), f32),
            pltpu.VMEM((STEPS, UNIT, 128), f32),
            pltpu.SemaphoreType.DMA((3,)),
            pltpu.SemaphoreType.DMA((3,)),
            pltpu.SemaphoreType.DMA((3,)),
            pltpu.SemaphoreType.DMA((7,)),
            pltpu.SemaphoreType.DMA((8,)),
            pltpu.SemaphoreType.DMA((6, STEPS)),
            pltpu.SemaphoreType.DMA((6, STEPS)),
            pltpu.SemaphoreType.DMA((1, STEPS)),
            pltpu.SemaphoreType.DMA((2, STEPS)),
        ],
        compiler_params=pltpu.CompilerParams(
            collective_id=0, has_side_effects=True, vmem_limit_bytes=48 * 2**20
        ),
        cost_estimate=pl.CostEstimate(
            flops=6 * 2304 * 576 * 576, bytes_accessed=3 * 2**20, transcendentals=0
        ),
        name="cycle_term",
    )(amplitudes.T, cycle_ints.T)
    return out.T


def solution(mesh):
    return jax.shard_map(
        per_device,
        mesh=mesh,
        in_specs=(P("row", ("col", "rep")), P(("col", "rep"), "row")),
        out_specs=P(("row", "rep"), "col"),
        check_vma=False,
    )
```

time: 520 us -> 104 us (0.20)
  the two profiles are of different devices: /device:TPU:8 before, /device:TPU:40 now
where the time goes in v1:
time: 104 us; the launch traced here: 103 us
  Pallas kernels  100 us (96%)
  local copies, waits for them, and re-layouts  3.36 us (3%)
    pallas_call x1, Pallas kernels, per_device(): pl.pallas_call(kernel, out_shape=jax.ShapeDtypeStruct((72, 576), f32), in...  100 us
    unnamed x5, local copies, waits for them, and re-layouts  3.36 us

profile of v1, /device:TPU:40, one launch (start us, length us, event | category | flops | bytes accessed | tf_op | source)
XLA Modules:
  0.0 103.5 jit_solution(1936888503558677902)
XLA Ops:
  0.0 0.0 copy-start
  0.0 1.7 %copy-done = f32[2304,288]{0,1:T(8,128)S(1)} copy-done((f32[2304,288]{0,1:T(8,128)S(1)}, f32[2304,288]{0,1:T(8,128)}, u32[]{:S(2)}) %copy-start) | copy-done | bytes 2654232
  1.8 0.0 copy-start.1
  1.8 0.9 copy-done.1
  2.7 100.1 %cycle_term.1 = f32[72,576]{1,0:T(8,128)S(1)} custom-call(f32[288,2304]{1,0:T(8,128)S(1)} %bitcast.4, f32[144,288]{1,0:T(8,128)S(1)} %bitcast.5), custom_call_target="tpu_custom_call" | custom-call | flops 4586471424 | bytes 3145728 | tf_op jit(solution)/shard_map/cycle_term/pallas_call | solution.py:292
  102.8 0.7 copy.4
Async XLA Ops:
  0.0 1.7 %copy-start = (f32[2304,288]{0,1:T(8,128)S(1)}, f32[2304,288]{0,1:T(8,128)}, u32[]{:S(2)}) copy-start(f32[2304,288]{0,1:T(8,128)} %param.2) | copy-start | bytes 7962628
  1.8 0.9 copy-start.1

commit v2 on v1

v2 whole, which is shorter than its diff:
```python
import functools

import jax
import jax.numpy as jnp
from jax import lax
from jax.experimental import pallas as pl
from jax.experimental.pallas import tpu as pltpu
from jax.sharding import PartitionSpec as P

MESH = pl.DeviceIdType.MESH
STEPS = 8
NX = 4
TOP = 160
UNIT = 328
BOT = UNIT - TOP
PARTS = ((0, 88), (88, 80), (168, 80), (248, 80))
LAGS = (2, 1)
BASES = (5, 13)
TURNS = 12
ISSUED = (2, 3, 4, 4, 5, 7, 8)


def split(value):
    high = value.astype(jnp.bfloat16)
    return high, (value - high.astype(jnp.float32)).astype(jnp.bfloat16)


def kernel(
    at_ref, bt_ref, out_ref,
    a_own, a_oth, ah, al, b_own, b_oth, bq, pu, opp_l, opp_r, in_l, in_r, z_in,
    loc_sem, core_s, core_r, b_s, b_r, x_s, x_r, z_s, z_rs, z_ready, h_ready,
):
    row, col, x = lax.axis_index("row"), lax.axis_index("col"), lax.axis_index("rep")
    y, h = row // 2, row % 2
    z, c = col // 2, col % 2
    other = {"col": col + 1 - 2 * c}
    right, left, opp = (x + 1) % NX, (x + 3) % NX, (x + 2) % NX
    to_right, to_left = {"rep": right}, {"rep": left}
    twin_row = row + 1 - 2 * h
    y_rows = [(row + 2) % 8, (row + 6) % 8, (row + 4) % 8]
    spans = [pl.ds(pl.multiple_of(1152 * p, 128), 1152) for p in (1 - x // 2, x // 2)]

    load_b = pltpu.make_async_copy(bt_ref, b_own, loc_sem.at[2])
    load_b.start()
    load_a = [
        pltpu.make_async_copy(at_ref.at[:, span], a_own.at[:, span], loc_sem.at[n])
        for n, span in enumerate(spans)
    ]
    for cp in load_a:
        cp.start()

    barrier = pltpu.get_barrier_semaphore()

    def greet(device, sem=barrier):
        pl.semaphore_signal(sem, inc=1, device_id=device, device_id_type=MESH)

    greet(other)
    greet(to_right)
    greet(to_left)
    for r in y_rows:
        greet({"row": r})

    @pl.when(z < 7)
    def _():
        greet({"col": col + 2})

    @pl.when(h == 0)
    def _():
        greet({"row": twin_row})

    pl.semaphore_wait(barrier, 6 + jnp.minimum(z, 1) + h)

    @pl.when(z > 0)
    def _():
        greet({"col": col - 2}, z_ready)

    @pl.when(h == 1)
    def _():
        greet({"row": twin_row}, h_ready)

    load_b.wait()
    swap_b = pltpu.make_async_remote_copy(
        b_own.at[pl.ds((1 - c) * 72, 72)], b_oth, core_s.at[0], core_r.at[0],
        device_id=other, device_id_type=MESH,
    )
    swap_b.start()
    swap_a = []
    for n, span in enumerate(spans):
        load_a[n].wait()
        cp = pltpu.make_async_remote_copy(
            a_own.at[:, span], a_oth.at[:, span],
            core_s.at[1 + n], core_r.at[1 + n], device_id=other, device_id_type=MESH,
        )
        cp.start()
        swap_a.append(cp)
    swap_b.wait_recv()
    mine = jnp.concatenate([b_own[pl.ds(c * 72, 72), :], b_oth[...]], axis=1)
    for j in range(4):
        bq[row, 72 * j:72 * j + 72, :] = mine[:, 128 * j:128 * j + 128]
    bq[row, 288:328, :] = jnp.concatenate([mine[0:40, 512:576], mine[32:72, 512:576]], axis=1)

    def send_b(slot, target, sem):
        return pltpu.make_async_remote_copy(
            bq.at[slot], bq.at[slot], b_s.at[sem], b_r.at[slot],
            device_id={"row": target}, device_id_type=MESH,
        )

    to_twin = send_b(row, twin_row, 0)

    @pl.when(h == 1)
    def _():
        to_twin.start()

    sends_b = [send_b(row, r, 1 + n) for n, r in enumerate(y_rows)]
    for cp in sends_b:
        cp.start()
    relays_b = [send_b(twin_row, r, 4 + n) for n, r in enumerate(y_rows)]

    def convert(source, base, n):
        span = spans[n]

        def some(i, _):
            rows = pl.ds(pl.multiple_of(i * 16, 16), 16)
            into = pl.ds(pl.multiple_of(base + i * 16, 16), 16)
            high, low = split(source[rows, span])
            ah[into, span] = high
            al[into, span] = low
            return 0

        lax.fori_loop(0, 18, some, 0, unroll=6)

    def by_distance(parity, first):
        blocks = [2 * a + parity for a in range(4)]
        keys = [
            2 * jnp.abs(d - z) + jnp.where(d > z, 1, 0) + jnp.where(d == first, 100, 0) for d in blocks
        ]
        ranks = [sum(jnp.where(other > key, 1, 0) for other in keys) for key in keys]
        return [sum(jnp.where(r == j, d, 0) for r, d in zip(ranks, blocks)) for j in range(4)]

    listed = by_distance(h, row) + by_distance(1 - h, twin_row)

    def order(i):
        d = listed[0]
        for n in range(1, STEPS):
            d = jnp.where(i == n, listed[n], d)
        return d

    lanes = lax.broadcasted_iota(jnp.int32, (40, 128), 1)

    def x_copy(kind, i):
        top, bot = pl.ds(0, TOP), pl.ds(TOP, BOT)
        src, dst, device = (
            (pu.at[i, opp, top], opp_l.at[i], to_right),
            (pu.at[i, opp, bot], opp_r.at[i], to_left),
            (pu.at[i, right, bot], in_l.at[i, bot], to_right),
            (pu.at[i, left, top], in_r.at[i, top], to_left),
            (pu.at[i, right, top], in_l.at[i, top], to_right),
            (pu.at[i, left, bot], in_r.at[i, bot], to_left),
        )[kind]
        return pltpu.make_async_remote_copy(
            src, dst, x_s.at[kind, i], x_r.at[kind, i], device_id=device, device_id_type=MESH
        )

    def z_copy(down, d, piece):
        part = pl.ds(*PARTS[piece])
        return pltpu.make_async_remote_copy(
            pu.at[d, x, part], z_in.at[down, d, part], z_s.at[piece, d], z_rs.at[piece, down, d],
            device_id={"col": col + 2 - 4 * down}, device_id_type=MESH,
        )

    def z_add(down, d, piece):
        part = slice(PARTS[piece][0], sum(PARTS[piece]))
        z_copy(down, d, piece).wait_recv()
        pu[d, x, part, :] += z_in[down, d, part, :]

    def half_product(i, b_parts, n):
        bh, bl = b_parts
        p = x // 2 if n else 1 - x // 2
        span = spans[n]
        high = ah[:, span]
        v = jnp.dot(bh, high, preferred_element_type=jnp.float32)
        v += jnp.dot(bl, high, preferred_element_type=jnp.float32)
        v += jnp.dot(bh, al[:, span], preferred_element_type=jnp.float32)
        for j in range(4):
            pu[i, 2 * p, 72 * j:72 * j + 72, :] = v[:, 128 * j:128 * j + 128]
            pu[i, 2 * p + 1, 72 * j:72 * j + 72, :] = v[:, 640 + 128 * j:768 + 128 * j]
        up, down = v[0:40, 512:640], v[32:72, 512:640]
        pu[i, 2 * p, 288:328, :] = jnp.where(lanes < 64, up, pltpu.roll(down, 64, 1))
        pu[i, 2 * p + 1, 288:328, :] = jnp.where(lanes < 64, pltpu.roll(up, 64, 1), down)
        x_copy(2 * n, i).start()
        x_copy(2 * n + 1, i).start()

    def b_of(d):
        tail = bq[d, 288:328, :]
        tail = jnp.concatenate([tail, pltpu.roll(tail, 64, 1)[8:40]], axis=0)
        tiles = [bq[d, 72 * j:72 * j + 72, :] for j in range(4)]
        return split(jnp.concatenate(tiles + [tail[:, 0:64]], axis=1))

    def product(d):
        @pl.when((d != row) & (d != twin_row))
        def _():
            send_b(d, twin_row, 0).wait_recv()

        parts = b_of(d)
        half_product(d, parts, 0)
        half_product(d, parts, 1)

    def relay(i):
        x_copy(0, i).wait_recv()
        pu[i, right, 0:TOP, :] += opp_l[i]
        x_copy(4, i).start()
        x_copy(1, i).wait_recv()
        pu[i, left, TOP:UNIT, :] += opp_r[i]
        x_copy(5, i).start()

    def gather(i):
        for kind in (2, 4, 3, 5):
            x_copy(kind, i).wait_recv()
        pu[i, x] += in_l[i] + in_r[i]

    def write_out(i):
        v = [pu[i, x, 72 * j:72 * j + 72, :] for j in range(4)]
        tail = pu[i, x, 288:328, :]
        tail = jnp.concatenate([tail, pltpu.roll(tail, 64, 1)[8:40]], axis=0)

        @pl.when(x % 2 == 0)
        def _():
            for j in range(4):
                out_ref[:, 128 * j:128 * j + 128] = v[j]
            out_ref[:, 512:576] = tail[:, 0:64]

        @pl.when(x % 2 == 1)
        def _():
            r = [pltpu.roll(w, 64, 1) for w in v]
            low = lax.broadcasted_iota(jnp.int32, (72, 128), 1) < 64
            out_ref[:, 0:128] = jnp.where(low, tail, r[0])
            for j in range(1, 4):
                out_ref[:, 128 * j:128 * j + 128] = jnp.where(low, r[j - 1], r[j])
            out_ref[:, 512:576] = r[3][:, 0:64]

    def z_tasks(slot):
        def one(i, _):
            d = order(i)
            down = jnp.where(d < z, 1, 0)
            hop = jnp.where(d < z, 7 - z, z)
            late = jnp.where(i < 4, BASES[0] + LAGS[0] * hop, BASES[1] + LAGS[1] * hop)
            late += jnp.where(i % 4 > 0, 2, 0)

            @pl.when((d != z) & (jnp.maximum(2 * i + 5, late) == slot))
            def _():
                for piece in range(len(PARTS)):
                    @pl.when(hop > 0)
                    def _():
                        z_add(down, d, piece)

                    z_copy(down, d, piece).start()

            return 0

        lax.fori_loop(0, STEPS, one, 0)

    def valid(i):
        return (i >= 0) & (i < STEPS)

    convert(a_own, 0, 0)
    convert(a_own, 0, 1)
    first_b = b_of(row)
    for n in range(2):
        swap_a[n].wait_recv()
        convert(a_oth, 288, n)
        half_product(row, first_b, n)

    @pl.when(z < 7)
    def _():
        pl.semaphore_wait(z_ready, 1)

    def issued(s):
        count = 1
        for turn, n in enumerate(ISSUED):
            count = jnp.where(s >= turn, n, count)
        return count

    def step(s, _):
        @pl.when(valid(s - 1))
        def _():
            relay(order(s - 1))

        @pl.when((s == 1) & (h == 0))
        def _():
            pl.semaphore_wait(h_ready, 1)
            to_twin.start()

        @pl.when(s == 4 - h)
        def _():
            send_b(twin_row, y_rows[0], 0).wait_recv()
            for cp in relays_b:
                cp.start()

        def some(i, _):
            product(order(i))
            return 0

        lax.fori_loop(issued(s - 1), issued(s), some, 0)

        z_tasks(2 * s)

        @pl.when(valid(s - 2))
        def _():
            gather(order(s - 2))

        z_tasks(2 * s + 1)
        return 0

    lax.fori_loop(0, TURNS, step, 0)

    for piece in range(len(PARTS)):
        @pl.when(z > 0)
        def _():
            z_add(0, z, piece)

        @pl.when(z < 7)
        def _():
            z_add(1, z, piece)

    write_out(z)

    def drain(i, _):
        for kind in range(6):
            x_copy(kind, i).wait_send()

        @pl.when(i != z)
        def _():
            for piece in range(len(PARTS)):
                z_copy(0, i, piece).wait_send()

        return 0

    lax.fori_loop(0, STEPS, drain, 0)
    swap_b.wait_send()
    for cp in swap_a:
        cp.wait_send()
    to_twin.wait_send()
    for cp in sends_b + relays_b:
        cp.wait_send()


def per_device(amplitudes, cycle_ints):
    f32 = jnp.float32
    out = pl.pallas_call(
        kernel,
        out_shape=jax.ShapeDtypeStruct((72, 576), f32),
        in_specs=[pl.BlockSpec(memory_space=pl.ANY)] * 2,
        out_specs=pl.BlockSpec(memory_space=pltpu.VMEM),
        scratch_shapes=[
            pltpu.VMEM((288, 2304), f32),
            pltpu.VMEM((288, 2304), f32),
            pltpu.VMEM((576, 2304), jnp.bfloat16),
            pltpu.VMEM((576, 2304), jnp.bfloat16),
            pltpu.VMEM((144, 288), f32),
            pltpu.VMEM((72, 288), f32),
            pltpu.VMEM((8, UNIT, 128), f32),
            pltpu.VMEM((STEPS, NX, UNIT, 128), f32),
            pltpu.VMEM((STEPS, TOP, 128), f32),
            pltpu.VMEM((STEPS, BOT, 128), f32),
            pltpu.VMEM((STEPS, UNIT, 128), f32),
            pltpu.VMEM((STEPS, UNIT, 128), f32),
            pltpu.VMEM((2, STEPS, UNIT, 128), f32),
            pltpu.SemaphoreType.DMA((3,)),
            pltpu.SemaphoreType.DMA((3,)),
            pltpu.SemaphoreType.DMA((3,)),
            pltpu.SemaphoreType.DMA((7,)),
            pltpu.SemaphoreType.DMA((8,)),
            pltpu.SemaphoreType.DMA((6, STEPS)),
            pltpu.SemaphoreType.DMA((6, STEPS)),
            pltpu.SemaphoreType.DMA((len(PARTS), STEPS)),
            pltpu.SemaphoreType.DMA((len(PARTS), 2, STEPS)),
            pltpu.SemaphoreType.REGULAR,
            pltpu.SemaphoreType.REGULAR,
        ],
        compiler_params=pltpu.CompilerParams(
            collective_id=0, has_side_effects=True, vmem_limit_bytes=60 * 2**20
        ),
        cost_estimate=pl.CostEstimate(
            flops=6 * 2304 * 576 * 576, bytes_accessed=3 * 2**20, transcendentals=0
        ),
        name="cycle_term",
    )(amplitudes.T, cycle_ints.T)
    return out.T


def solution(mesh):
    return jax.shard_map(
        per_device,
        mesh=mesh,
        in_specs=(P("row", ("col", "rep")), P(("col", "rep"), "row")),
        out_specs=P(("row", "rep"), "col"),
        check_vma=False,
    )
```

time: 104 us -> 83.8 us (0.81)
  the two profiles are of different devices: /device:TPU:40 before, /device:TPU:96 now
where the time goes in v2:
time: 83.8 us; the launch traced here: 83.6 us
  Pallas kernels  82 us (98%)
  local copies, waits for them, and re-layouts  1.61 us (2%)
    pallas_call x1, Pallas kernels, per_device(): pl.pallas_call(kernel, out_shape=jax.ShapeDtypeStruct((72, 576), f32), in...  82 us

profile of v2, /device:TPU:96, one launch (start us, length us, event | category | flops | bytes accessed | tf_op | source)
XLA Modules:
  0.0 83.6 jit_solution(3713554188199126285)
XLA Ops:
  0.0 82.0 %cycle_term.1 = f32[72,576]{1,0:T(8,128)} custom-call(f32[288,2304]{1,0:T(8,128)} %bitcast.4, f32[144,288]{1,0:T(8,128)} %bitcast.5), custom_call_target="tpu_custom_call" | custom-call | flops 4586471424 | bytes 3145728 | tf_op jit(solution)/shard_map/cycle_term/pallas_call | solution.py:349
  82.0 1.6 %copy.4 = f32[576,72]{0,1:T(8,128)} copy(f32[576,72]{0,1:T(8,128)} %bitcast.3) | data formatting | bytes 331776

commit v3 on v2

--- a/solution.py
+++ b/solution.py
@@ -16,7 +16,7 @@
 PARTS = ((0, 88), (88, 80), (168, 80), (248, 80))
 LAGS = (2, 1)
 BASES = (5, 13)
-TURNS = 12
+TURNS = 11
 ISSUED = (2, 3, 4, 4, 5, 7, 8)
 
 
@@ -238,15 +238,22 @@
                 out_ref[:, 128 * j:128 * j + 128] = jnp.where(low, r[j - 1], r[j])
             out_ref[:, 512:576] = r[3][:, 0:64]
 
+    def due_of(i):
+        d, first = listed[i], (row if i < 4 else twin_row)
+        g = i // 4
+        lower = jnp.where(d < z, 1, 0)
+        ahead = jnp.where(d < z, d // 2, 3 - d // 2)
+        ahead += 1 - jnp.where(d < z, jnp.where(first < d, 1, 0), jnp.where(first > d, 1, 0))
+        start = BASES[g] + jnp.where(d == first, 0, 2 * ahead)
+        hop = jnp.where(d < z, 7 - z, z)
+        due = jnp.maximum(2 * i + 5, start + LAGS[g] * hop)
+        return lower, hop, jnp.where(d == z, -1, due)
+
+    dues = [due_of(i) for i in range(STEPS)]
+
     def z_tasks(slot):
-        def one(i, _):
-            d = order(i)
-            down = jnp.where(d < z, 1, 0)
-            hop = jnp.where(d < z, 7 - z, z)
-            late = jnp.where(i < 4, BASES[0] + LAGS[0] * hop, BASES[1] + LAGS[1] * hop)
-            late += jnp.where(i % 4 > 0, 2, 0)
-
-            @pl.when((d != z) & (jnp.maximum(2 * i + 5, late) == slot))
+        for d, (down, hop, due) in zip(listed, dues):
+            @pl.when(due == slot)
             def _():
                 for piece in range(len(PARTS)):
                     @pl.when(hop > 0)
@@ -254,10 +261,6 @@
                         z_add(down, d, piece)
 
                     z_copy(down, d, piece).start()
-
-            return 0
-
-        lax.fori_loop(0, STEPS, one, 0)
 
     def valid(i):
         return (i >= 0) & (i < STEPS)
@@ -290,7 +293,7 @@
             pl.semaphore_wait(h_ready, 1)
             to_twin.start()
 
-        @pl.when(s == 4 - h)
+        @pl.when(s == 3 + h)
         def _():
             send_b(twin_row, y_rows[0], 0).wait_recv()
             for cp in relays_b:
@@ -313,35 +316,40 @@
 
     lax.fori_loop(0, TURNS, step, 0)
 
-    for piece in range(len(PARTS)):
-        @pl.when(z > 0)
-        def _():
-            z_add(0, z, piece)
-
-        @pl.when(z < 7)
-        def _():
-            z_add(1, z, piece)
-
-    write_out(z)
-
-    def drain(i, _):
+    def drain_x(i, _):
         for kind in range(6):
             x_copy(kind, i).wait_send()
 
-        @pl.when(i != z)
-        def _():
-            for piece in range(len(PARTS)):
-                z_copy(0, i, piece).wait_send()
-
         return 0
 
-    lax.fori_loop(0, STEPS, drain, 0)
+    lax.fori_loop(0, STEPS, drain_x, 0)
     swap_b.wait_send()
     for cp in swap_a:
         cp.wait_send()
     to_twin.wait_send()
     for cp in sends_b + relays_b:
         cp.wait_send()
+
+    for piece in range(len(PARTS)):
+        @pl.when(z > 0)
+        def _():
+            z_add(0, z, piece)
+
+        @pl.when(z < 7)
+        def _():
+            z_add(1, z, piece)
+
+    write_out(z)
+
+    def drain_z(i, _):
+        @pl.when(i != z)
+        def _():
+            for piece in range(len(PARTS)):
+                z_copy(0, i, piece).wait_send()
+
+        return 0
+
+    lax.fori_loop(0, STEPS, drain_z, 0)
 
 
 def per_device(amplitudes, cycle_ints):

time: 83.8 us -> 83.1 us (level)
  the two profiles are of different devices: /device:TPU:96 before, /device:TPU:54 now
where the time goes in v3:
time: 83.1 us; the launch traced here: 82.9 us
  Pallas kernels  81.3 us (98%)
  local copies, waits for them, and re-layouts  1.61 us (2%)
    pallas_call x1, Pallas kernels, per_device(): pl.pallas_call(kernel, out_shape=jax.ShapeDtypeStruct((72, 576), f32), in...  81.3 us

profile of v3, /device:TPU:54, one launch (start us, length us, event | category | flops | bytes accessed | tf_op | source)
XLA Modules:
  0.0 82.9 jit_solution(6230700901312282437)
XLA Ops:
  0.0 81.3 %cycle_term.1 = f32[72,576]{1,0:T(8,128)} custom-call(f32[288,2304]{1,0:T(8,128)} %bitcast.4, f32[144,288]{1,0:T(8,128)} %bitcast.5), custom_call_target="tpu_custom_call" | custom-call | flops 4586471424 | bytes 3145728 | tf_op jit(solution)/shard_map/cycle_term/pallas_call | solution.py:357
  81.3 1.6 %copy.4 = f32[576,72]{0,1:T(8,128)} copy(f32[576,72]{0,1:T(8,128)} %bitcast.3) | data formatting | bytes 331776

commit v4 on v3

--- a/solution.py
+++ b/solution.py
@@ -13,7 +13,7 @@
 TOP = 160
 UNIT = 328
 BOT = UNIT - TOP
-PARTS = ((0, 88), (88, 80), (168, 80), (248, 80))
+PARTS = tuple((40 * n, 40) for n in range(7)) + ((280, 48),)
 LAGS = (2, 1)
 BASES = (5, 13)
 TURNS = 11

time: 83.1 us -> 82.8 us (level)
  no operation moved by 1% of the time
where the time goes in v4:
time: 82.8 us; the launch traced here: 82.7 us
  Pallas kernels  81 us (98%)
  local copies, waits for them, and re-layouts  1.61 us (2%)
    pallas_call x1, Pallas kernels, per_device(): pl.pallas_call(kernel, out_shape=jax.ShapeDtypeStruct((72, 576), f32), in...  81 us

profile of v4, /device:TPU:54, one launch (start us, length us, event | category | flops | bytes accessed | tf_op | source)
XLA Modules:
  0.0 82.7 jit_solution(1956483112063746525)
XLA Ops:
  0.0 81.0 %cycle_term.1 = f32[72,576]{1,0:T(8,128)} custom-call(f32[288,2304]{1,0:T(8,128)} %bitcast.4, f32[144,288]{1,0:T(8,128)} %bitcast.5), custom_call_target="tpu_custom_call" | custom-call | flops 4586471424 | bytes 3145728 | tf_op jit(solution)/shard_map/cycle_term/pallas_call | solution.py:357
  81.1 1.6 %copy.4 = f32[576,72]{0,1:T(8,128)} copy(f32[576,72]{0,1:T(8,128)} %bitcast.3) | data formatting | bytes 331776
